TPU v7x, 128 devices: a whole 4x4x4 slice. The times are simulated.
128 devices in a mesh: section: 2 (over core), ctx: 64 (over z, x, y).
Axes of the slice: x: 4, y: 4, z: 4, core: 2. Of those that a mesh axis runs over, the one named last changes fastest.
Arguments:
- queries: bfloat16 [2, 32768, 2048], P('section', 'ctx'), may hold values from -20 to 20
- nb_kv: bfloat16 [2, 512, 2, 128, 1024], P('section', 'ctx'), may hold values from -6 to 6
- out_grad: bfloat16 [32768, 2048], P('ctx'), may hold values from -6 to 6
- kv_weight: bfloat16 [2, 896, 1024], P('section'), may hold values from -0.1875 to 0.1875
- nb_owner: int32 [512, 2], P('ctx'), may hold values from 0 to 63, all different within a row; in each aligned block of 8 rows (0 to 7, 8 to 15, ...) at most 2 rows name the same one
- nb_row: int32 [512, 2], P('ctx'), may hold values from 0 to 15
Outputs:
- input_grads: bfloat16 [2, 32768, 2048], P('section', 'ctx')
- enc_grad: bfloat16 [1024, 128, 896], P('ctx', None, 'section')
Inputs may be any that keep to these rules, and one draw needn't show every extreme that they name: `nb_owner`: the 2 neighbours of a span have different owners. Among the spans of one device (aligned blocks of 8 spans) no owner is named more than 2 times, a bound that some block reaches.
All inputs are finite; a program needn't handle non-finite values.
Results may differ from a plain program's by a relative error of at most 0.0076.
Values may be sent and summed in bfloat16 or wider, within the bound.
A program may use at most 192 MiB of HBM per device.

v0:
```python
import math

import jax
import jax.numpy as jnp
from jax import lax
from jax.sharding import PartitionSpec as P

HEADS = 16
KV_HEADS = 4
HDIM = 128
SPAN = 64
NB = 2
NBLEN = 128
CAP = 2


def from_behind(value, axis, steps):
    count = lax.axis_size(axis)
    leading, last = (max(0, -steps), min(count, count - steps))
    return lax.ppermute(value, axis, [(source, source + steps) for source in range(leading, last)])


def span_backward(query_rows, cotangent, neighbour_kv):
    span_total = query_rows.shape[0]
    kv_width = neighbour_kv.shape[-1] // 2
    group_size = HEADS // KV_HEADS
    score_scale = 1.0 / math.sqrt(HDIM)
    query_heads = query_rows.reshape(span_total, SPAN, KV_HEADS, group_size, HDIM)
    grad_heads = cotangent.reshape(span_total, SPAN, KV_HEADS, group_size, HDIM)
    key_rows = neighbour_kv[..., :kv_width].reshape(span_total, NB * NBLEN, KV_HEADS, HDIM)
    value_rows = neighbour_kv[..., kv_width:].reshape(span_total, NB * NBLEN, KV_HEADS, HDIM)
    scores = (
        jnp.einsum("cqhgd,ckhd->chgqk", query_heads, key_rows, preferred_element_type=jnp.float32)
        * score_scale
    )
    row_peak = jnp.max(scores, axis=-1, keepdims=True)
    weights_raw = jnp.exp(scores - row_peak)
    probabilities = weights_raw / jnp.sum(weights_raw, axis=-1, keepdims=True)
    probs_low = probabilities.astype(jnp.bfloat16)
    outputs = jnp.einsum(
        "chgqk,ckhd->cqhgd", probs_low, value_rows, preferred_element_type=jnp.float32
    )
    row_dot = jnp.sum(grad_heads.astype(jnp.float32) * outputs, axis=-1)
    value_grad = jnp.einsum(
        "chgqk,cqhgd->ckhd", probs_low, grad_heads, preferred_element_type=jnp.float32
    )
    prob_grad = jnp.einsum(
        "cqhgd,ckhd->chgqk", grad_heads, value_rows, preferred_element_type=jnp.float32
    )
    score_grad = (
        probabilities * (prob_grad - jnp.transpose(row_dot, (0, 2, 3, 1))[..., None])
    ).astype(jnp.bfloat16)
    query_grad = (
        jnp.einsum("chgqk,ckhd->cqhgd", score_grad, key_rows, preferred_element_type=jnp.float32)
        * score_scale
    )
    key_grad = (
        jnp.einsum("chgqk,cqhgd->ckhd", score_grad, query_heads, preferred_element_type=jnp.float32)
        * score_scale
    )
    input_grad = (cotangent.astype(jnp.float32) + query_grad.reshape(span_total, SPAN, -1)).astype(
        jnp.bfloat16
    )
    kv_grad = jnp.concatenate(
        [
            key_grad.reshape(span_total, NB, NBLEN, kv_width),
            value_grad.reshape(span_total, NB, NBLEN, kv_width),
        ],
        axis=-1,
    ).astype(jnp.bfloat16)
    return (input_grad, kv_grad)


def group_backward(packed):
    return span_backward(packed[0], packed[1], packed[2])


def run_block(query_block, grad_block, kv_block):
    span_total = kv_block.shape[0]
    group_size = math.gcd(span_total, 4)
    block_count = span_total // group_size
    query_groups = query_block.reshape(block_count, group_size, SPAN, -1)
    grad_groups = grad_block.reshape(block_count, group_size, SPAN, -1)
    kv_groups = kv_block.reshape((block_count, group_size) + kv_block.shape[1:])
    grad_part, kv_part = lax.map(group_backward, (query_groups, grad_groups, kv_groups))
    return (grad_part.reshape(query_block.shape), kv_part.reshape(kv_block.shape))


def earlier_slots(owner_lists):
    item_count = owner_lists.shape[-1]
    item_order = jnp.arange(item_count)
    earlier = item_order[None, :] < item_order[:, None]
    same_owner = owner_lists[..., :, None] == owner_lists[..., None, :]
    return jnp.sum(same_owner & earlier, axis=-1)


def local(queries, nb_kv, out_grad, kv_weight, nb_owner, nb_row):
    sections = lax.axis_size("section")
    devices = lax.axis_size("ctx")
    section_index = lax.axis_index("section")
    my_queries = queries[0]
    my_kv = nb_kv[0]
    span_count = my_kv.shape[0]
    incoming = out_grad
    input_grad = jnp.zeros_like(out_grad)
    kv_grads = jnp.zeros_like(my_kv)
    for round_index in range(sections):
        grad_block, kv_block = run_block(my_queries, incoming, my_kv)
        owned_now = section_index == sections - 1 - round_index
        input_grad = jnp.where(owned_now, grad_block, input_grad)
        kv_grads = jnp.where(owned_now, kv_block, kv_grads)
        if round_index + 1 < sections:
            incoming = from_behind(grad_block, "section", -1)
    item_count = span_count * NB
    slot_count = devices * CAP
    kv_flat = kv_grads.reshape(item_count, -1)
    owners_all, rows_all = (
        lax.all_gather(nb_owner, "ctx", axis=0, tiled=True),
        lax.all_gather(nb_row, "ctx", axis=0, tiled=True),
    )
    owners_all = owners_all.reshape(devices, item_count)
    rows_all = rows_all.reshape(devices, item_count)
    my_index = lax.axis_index("ctx")
    own_owner = nb_owner.reshape(-1)
    destination = own_owner * CAP + earlier_slots(own_owner)
    send_table = jnp.arange(slot_count)[:, None] == destination[None, :]
    target_all = jnp.arange(devices)[:, None] * CAP + earlier_slots(owners_all)
    source_slot = jnp.where(owners_all == my_index, target_all, -1).reshape(-1)
    local_row = rows_all.reshape(-1)
    row_match = (local_row[:, None] == jnp.arange(item_count)[None, :]) & (source_slot >= 0)[
        :, None
    ]
    slot_match = source_slot[:, None] == jnp.arange(slot_count)[None, :]
    recv_table = lax.dot_general(
        row_match.astype(jnp.float32), slot_match.astype(jnp.float32), (((0,), (0,)), ((), ()))
    ).astype(jnp.bfloat16)
    send_buffer = jnp.dot(
        send_table.astype(jnp.bfloat16), kv_flat, preferred_element_type=jnp.bfloat16
    )
    send_buffer = send_buffer.reshape(devices, CAP, NBLEN, -1)
    weight_wide = kv_weight[0].astype(jnp.float32)
    received_slots = lax.all_to_all(send_buffer, "ctx", split_axis=0, concat_axis=0, tiled=True)
    token_count = received_slots.shape[2]
    summed = jnp.dot(
        recv_table, received_slots.reshape(slot_count, -1), preferred_element_type=jnp.float32
    )
    projected = lax.dot_general(
        summed.reshape(item_count * token_count, -1),
        weight_wide,
        (((1,), (1,)), ((), ())),
        precision=lax.Precision.HIGHEST,
    )
    encoder_grad = projected.reshape(item_count, token_count, -1)
    layer_sum = lax.psum_scatter(
        encoder_grad.astype(jnp.bfloat16), "section", scatter_dimension=2, tiled=True
    )
    return (input_grad[None], layer_sum)


def solution(mesh):
    in_specs = (
        P("section", "ctx", None),
        P("section", "ctx", None, None, None),
        P("ctx", None),
        P("section", None, None),
        P("ctx", None),
        P("ctx", None),
    )
    out_specs = (P("section", "ctx", None), P("ctx", None, "section"))
    return jax.shard_map(local, mesh=mesh, in_specs=in_specs, out_specs=out_specs, check_vma=False)
```

profile of v0, /device:TPU:0, one launch (start us, length us, event | category | flops | bytes accessed | tf_op | source)
XLA Modules:
  0.0 1419.6 jit_solution(12873676765953113657)
XLA Ops:
  8.7 4.1 broadcast.139.clone
  12.9 122.5 %while.24 = (s32[]{:T(128)}, bf16[2,4,64,2048]{3,2,1,0:T(8,128)(2,1)}, bf16[2,4,2,128,1024]{3,2,4,1,0:T(2,128)(2,1)}, bf16[2,4,64,2048]{3,2,1,0:T(8,128)(2,1)}, ...) while((s32[]{:T(128)}, bf16[2,4,64,2048]{3,2,1,0:T(8,128)(2,1)}, ...), condition=%wide.region_4.5_spmd, body=%wide.region_0.4_spmd.sunk | while | flops 1630531840 | bytes 152125776 | solution.py:85
  17.7 3.2 constant_dynamic-slice_fusion.6
  25.4 11.1 fusion.142
  43.8 3.1 fusion.144
  54.3 3.1 reshape.301
  57.4 3.3 fusion.146
  64.3 3.2 fusion.148
  69.8 4.4 maximum_dynamic-update-slice_fusion.4
  78.8 3.2 constant_dynamic-slice_fusion.6
  86.5 11.1 fusion.142
  105.0 3.1 fusion.144
  115.4 3.1 reshape.301
  118.5 3.3 fusion.146
  125.5 3.2 fusion.148
  131.0 4.3 maximum_dynamic-update-slice_fusion.4
  137.2 4.5 collective-permute-done
  143.3 4.1 broadcast.139
  147.4 123.2 %while.25 = (s32[]{:T(128)}, bf16[2,4,64,2048]{3,2,1,0:T(8,128)(2,1)}, bf16[2,4,2,128,1024]{3,2,4,1,0:T(2,128)(2,1)}, bf16[2,4,64,2048]{3,2,1,0:T(8,128)(2,1)}, ...) while((s32[]{:T(128)}, bf16[2,4,64,2048]{3,2,1,0:T(8,128)(2,1)}, ...), condition=%wide.region_9.10_spmd, body=%wide.region_5.9_spmd.sunk | while | flops 1630531840 | bytes 152125776 | solution.py:85
  152.1 3.1 constant_dynamic-slice_fusion.7
  159.7 11.1 fusion.163
  178.3 3.1 fusion.165
  181.7 3.0 fusion.166
  188.7 3.1 reshape.306
  191.8 3.3 fusion.167
  198.9 3.2 fusion.169
  204.4 4.4 maximum_dynamic-update-slice_fusion.5
  213.5 3.1 constant_dynamic-slice_fusion.7
  221.1 11.1 fusion.163
  239.7 3.1 fusion.165
  243.1 3.0 fusion.166
  250.1 3.1 reshape.306
  253.2 3.3 fusion.167
  260.3 3.2 fusion.169
  265.8 4.4 maximum_dynamic-update-slice_fusion.5
  270.6 9.0 broadcast_select_fusion.1
  279.6 11.2 copy.125
  290.8 16.0 %fusion.52 = bf16[64,2,128,1024]{3,0,2,1:T(8,128)(2,1)} fusion(s32[64,2]{0,1:T(2,128)S(1)} %multiply_add_fusion, s32[16]{0:T(128)S(1)} %multiply_add_fusion.1, bf16[2,8,128,1024]{3,2,1,0:T(8,128)(2,1)} %bitcast.253), kind=kOutput, calls=%fused_computation.77 | convolution fusion | flops 536872960 | bytes 37749312 | tf_op jit(solution)/shard_map/dot_general | solution.py:137
  306.8 30.8 %copy.127 = bf16[64,2,128,1024]{3,2,1,0:T(8,128)(2,1)} copy(bf16[64,2,128,1024]{3,0,2,1:T(8,128)(2,1)} %fusion.52) | data formatting | bytes 67108864 | tf_op jit(solution)/shard_map/dot_general | solution.py:137
  337.6 11.9 all-to-all-start
  349.5 768.7 %all-gather.1 = s32[64,8,2]{1,2,0:T(2,128)S(1)} all-gather(s32[1,8,2]{1,2,0:T(2,128)S(1)} %bitcast.257), channel_id=1, replica_groups=mesh['section'=2,'ctx'=64] {'ctx'}, dimensions={0}, use_global_device_ids=true | all-gather | bytes 4160 | tf_op jit(solution)/shard_map/all_gather | solution.py:118
  1119.1 169.3 %all-gather = s32[64,8,2]{1,2,0:T(2,128)S(1)} all-gather(s32[1,8,2]{1,2,0:T(2,128)S(1)} %bitcast.258), channel_id=1, replica_groups=mesh['section'=2,'ctx'=64] {'ctx'}, dimensions={0}, use_global_device_ids=true | all-gather | bytes 4160 | tf_op jit(solution)/shard_map/all_gather | solution.py:119
  1289.0 30.8 %copy.161 = bf16[16,8,128,1024]{3,1,2,0:T(8,128)(2,1)} copy(bf16[16,8,128,1024]{3,2,1,0:T(8,128)(2,1)} %bitcast.73) | data formatting | bytes 67108864
  1319.9 43.9 %copy.128 = bf16[131072,128]{1,0:T(8,128)(2,1)} copy(bf16[131072,128]{0,1:T(8,128)(2,1)} %bitcast.245) | data formatting | bytes 67108864 | tf_op jit(solution)/shard_map/dot_general | solution.py:144
  1363.8 19.3 %fusion.59 = f32[16,128,1024]{2,0,1:T(8,128)} fusion(bf16[128,1024,128]{2,1,0:T(8,128)(2,1)} %bitcast.244, s32[1024]{0:T(1024)S(1)} %get-tuple-element.97, s32[1024]{0:T(1024)S(1)} %eq.105, pred[1024]{0:T(1024)(128)(4,1)S(1)} %get-tuple-element.96), kind=kOutput, calls=%fused_computation.84 | convolution fusion | flops 541231104 | bytes 41952256 | tf_op jit(solution)/shard_map/dot_general | solution.py:144
  1383.1 19.8 %fusion.54 = bf16[16,128,896]{1,2,0:T(8,128)(2,1)} fusion(f32[16,128,1024]{2,0,1:T(8,128)} %fusion.59, bf16[1,896,1024]{2,1,0:T(8,128)(2,1)S(1)} %copy-done), kind=kOutput, calls=%fused_computation.79 | convolution fusion | flops 22550413312 | bytes 13893632 | tf_op jit(solution)/shard_map/dot_general | solution.py:147
  1403.0 3.1 select_select_fusion
  1406.1 6.5 reduce-scatter.2.cloned.1.call-done
  (143 shorter events, 119.9 us)
Async XLA Ops:
  7.2 1375.9 %copy-start = (bf16[1,896,1024]{2,1,0:T(8,128)(2,1)S(1)}, bf16[1,896,1024]{2,1,0:T(8,128)(2,1)}, u32[]{:S(2)}) copy-start(bf16[1,896,1024]{2,1,0:T(8,128)(2,1)} %param.13) | copy-start | bytes 5505028
  12.8 124.0 %copy-start.15 = (s32[8,2]{0,1:T(2,128)S(1)}, s32[8,2]{0,1:T(2,128)}, u32[]{:S(2)}) copy-start(s32[8,2]{0,1:T(2,128)} %param.14) | copy-start | bytes 196
  36.5 2.6 copy-start.1
  43.8 3.4 copy-start.2
  50.2 1.3 copy-start.9
  57.4 3.3 copy-start.7
  57.4 3.3 copy-start.13
  60.6 3.7 copy-start.5
  67.6 2.2 copy-start.11
  97.7 2.6 copy-start.1
  105.0 3.4 copy-start.2
  111.4 1.3 copy-start.9
  118.5 3.3 copy-start.7
  118.5 3.3 copy-start.13
  121.8 3.7 copy-start.5
  128.7 2.2 copy-start.11
  135.3 6.4 collective-permute-start
  170.9 2.6 copy-start.3
  178.3 3.4 copy-start.4
  184.7 1.3 copy-start.10
  191.8 3.3 copy-start.8
  191.8 3.3 copy-start.14
  196.7 2.3 copy-start.6
  202.1 2.3 copy-start.12
  232.3 2.6 copy-start.3
  239.6 3.4 copy-start.4
  246.1 1.3 copy-start.10
  253.2 3.3 copy-start.8
  253.2 3.3 copy-start.14
  258.1 2.3 copy-start.6
  263.5 2.3 copy-start.12
  337.5 12.0 copy-start.16
  337.5 781.5 %copy-start.17 = (s32[8,2]{0,1:T(2,128)S(1)}, s32[8,2]{0,1:T(2,128)}, u32[]{:S(2)}) copy-start(s32[8,2]{0,1:T(2,128)} %param.15) | copy-start | bytes 196
  337.6 951.5 %all-to-all-start = ((bf16[64,2,128,1024]{3,2,1,0:T(8,128)(2,1)}), bf16[64,2,128,1024]{3,2,1,0:T(8,128)(2,1)}, u32[]{:S(2)}, u32[]{:S(2)}) async-start(bf16[64,2,128,1024]{3,2,1,0:T(8,128)(2,1)} %copy.127), calls=%async_computation | async-start | bytes 67108864 | tf_op jit(solution)/shard_map/all_to_all | solution.py:142
  349.5 1063.1 %reduce-scatter.2.cloned.1.call-start = ((), (), s32[]{:S(2)}) async-start(), calls=%async_computation.2 | async-start | bytes 5505024 | tf_op jit(solution)/shard_map/reduce_scatter | solution.py:154
Sparse Core Ops, SparseCore 0:
  1403.1 9.4 reduce-scatter.1
where the time goes:
time: 1430 us; the launch traced here: 1420 us
  blocking collectives  938 us (66%)
  local copies, waits for them, and re-layouts  236 us (17%)
  matrix products  109 us (8%)
  other arithmetic  96.2 us (7%)
  between operations  14.3 us (1%)
    all_gather x1, blocking collectives, local(): lax.all_gather(nb_owner, 'ctx', axis=0, tiled=True)  769 us
    all_gather x1, blocking collectives, local(): lax.all_gather(nb_row, 'ctx', axis=0, tiled=True)  169 us
    sub x4, other arithmetic, span_backward(): weights_raw = jnp.exp(scores - row_peak)  44.5 us
    dot_general x1, local copies, waits for them, and re-layouts, local(): jnp.dot(recv_table, received_slots.reshape(slot_count, -1), preferred_ele...  43.9 us
    unnamed x10, local copies, waits for them, and re-layouts  30.9 us
    dot_general x1, local copies, waits for them, and re-layouts, local(): jnp.dot(send_table.astype(jnp.bfloat16), kv_flat, preferred_element_type=...  30.8 us
    dynamic_update_slice x8, other arithmetic, run_block(): lax.map(group_backward, (query_groups, grad_groups, kv_groups))  30.5 us
  transfers between devices with their start and end apart: 3, of which 2 were waited for; matrix products, arithmetic and copies ran while one was open for 0% of the time, Pallas kernels for 0%

commit v1 on v0

v1 whole, which is shorter than its diff:
```python
import functools
import math

import jax
import jax.numpy as jnp
from jax import lax
from jax.experimental import pallas as pl
from jax.experimental.pallas import tpu as pltpu
from jax.sharding import PartitionSpec as P

HEADS = 16
KV_HEADS = 4
GROUP = HEADS // KV_HEADS
HDIM = 128
SPAN = 64
NB = 2
NBLEN = 128
CAP = 2
RING = 4
ROWS_DEV = 16
STRIDES = (16, 4, 1)
HALF = 448
PARTS = ((0, 160), (160, 144), (304, 144))
LAG_SUM = 2
LAG_FWD = 4
F32 = jnp.float32
BF16 = jnp.bfloat16
MESH = pl.DeviceIdType.MESH


def axis_step(axis, delta):
    me = lax.axis_index("ctx")
    stride = STRIDES[axis]
    coord = lax.rem(me // stride, RING)
    return me + (lax.rem(coord + delta + RING, RING) - coord) * stride


def greet(devices):
    barrier = pltpu.get_barrier_semaphore()
    for device in devices:
        pl.semaphore_signal(barrier, inc=1, device_id=device, device_id_type=MESH)
    pl.semaphore_wait(barrier, len(devices))


def neighbours():
    sec = lax.axis_index("section")
    return [[(sec, axis_step(a, 1)), (sec, axis_step(a, -1))] for a in range(3)]


def nt(a, b):
    return lax.dot_general(a, b, (((1,), (1,)), ((), ())), preferred_element_type=F32)


def nn(a, b):
    return lax.dot_general(a, b, (((1,), (0,)), ((), ())), preferred_element_type=F32)


def tn(a, b):
    return lax.dot_general(a, b, (((0,), (0,)), ((), ())), preferred_element_type=F32)


def pack_half(prod, n):
    base = n * NBLEN
    blocks = [prod[base : base + NBLEN, j * 128 : (j + 1) * 128] for j in range(3)]
    lane = lax.broadcasted_iota(jnp.int32, (NBLEN // 2, 128), 1)
    tail = jnp.where(
        lane < 64,
        prod[base : base + NBLEN // 2, 384:512],
        prod[base + NBLEN // 2 : base + NBLEN, 384:512],
    )
    return jnp.concatenate(blocks + [tail], axis=0)


def relay_kernel(
    q_hbm, kv_hbm, og_hbm, w_hbm, ig_hbm, gath_hbm,
    q_v, kv_v, cot_v, ig_v, w_v, kvg_v, own_v, xsend_v, xrecv_v, gown_v,
    ld_sem, w_sem, out_sem, cs_send, cs_recv, xs_send, xs_recv, gl_sem,
    ag_send, ag_recv, fw_send, fw_recv,
):
    spans = kv_v.shape[0]
    sec = lax.axis_index("section")
    me = lax.axis_index("ctx")
    partner = (1 - sec, me)
    near = neighbours()
    scale = 1.0 / math.sqrt(HDIM)

    def load(c, which):
        hbm, vmem = ((q_hbm, q_v), (kv_hbm, kv_v), (og_hbm, cot_v))[which]
        return pltpu.make_async_copy(hbm.at[c], vmem.at[c], ld_sem.at[c, which])

    def load_w(half, piece):
        if piece == 0:
            source, target = pl.ds(half * HALF, HALF), pl.ds(0, HALF)
        else:
            source, target = pl.ds(half * HALF + 384, 64), pl.ds(HALF, 64)
        return pltpu.make_async_copy(w_hbm.at[source], w_v.at[half, target], w_sem.at[half, piece])

    def out_copy(c):
        return pltpu.make_async_copy(ig_v.at[c], ig_hbm.at[c], out_sem.at[c])

    def cot_copy(c):
        return pltpu.make_async_remote_copy(
            ig_v.at[c], cot_v.at[c], cs_send.at[c], cs_recv.at[c], device_id=partner, device_id_type=MESH
        )

    def proj_copy(c):
        return pltpu.make_async_remote_copy(
            xsend_v.at[c], xrecv_v.at[c], xs_send.at[c], xs_recv.at[c], device_id=partner, device_id_type=MESH
        )

    def own_copy(c):
        return pltpu.make_async_copy(gown_v.at[c], gath_hbm.at[0, c], gl_sem.at[c])

    def gather_copy(c, p, way):
        rows = pl.ds(*PARTS[p])
        return pltpu.make_async_remote_copy(
            gown_v.at[c, :, rows], gath_hbm.at[1 + 2 * way, c, :, rows],
            ag_send.at[c, p, way], ag_recv.at[c, p, way], device_id=near[p][way], device_id_type=MESH,
        )

    def forward_copy(c, p, way):
        rows = pl.ds(*PARTS[p])
        return pltpu.make_async_remote_copy(
            gath_hbm.at[1 + 2 * way, c, way, rows], gath_hbm.at[2, c, way, rows],
            fw_send.at[c, p, way], fw_recv.at[c, p, way], device_id=near[p][way], device_id_type=MESH,
        )

    def start_loads(c, carry):
        load(c, 0).start()
        load(c, 1).start()

        @pl.when(sec == 1)
        def _():
            load(c, 2).start()

        return carry

    lax.fori_loop(0, 1, start_loads, 0)
    for half in range(2):
        for piece in range(2):
            load_w(half, piece).start()
    lax.fori_loop(1, spans, start_loads, 0)

    greet([partner] + [d for pair in near for d in pair])

    for half in range(2):
        for piece in range(2):
            load_w(half, piece).wait()

    def attend(c):
        for h in range(KV_HEADS):
            heads = [slice((h * GROUP + g) * HDIM, (h * GROUP + g + 1) * HDIM) for g in range(GROUP)]
            cols = slice(h * HDIM, (h + 1) * HDIM)
            vcols = slice((KV_HEADS + h) * HDIM, (KV_HEADS + h + 1) * HDIM)
            q = jnp.concatenate([q_v[c, :, s] for s in heads], axis=0)
            g = jnp.concatenate([cot_v[c, :, s] for s in heads], axis=0)
            k = kv_v[c, :, cols]
            v = kv_v[c, :, vcols]
            s = nt(k, q) * (scale * math.log2(math.e))
            e = jnp.exp2(s - jnp.max(s, axis=0, keepdims=True))
            prob = e * (1.0 / jnp.sum(e, axis=0, keepdims=True))
            low = prob.astype(BF16)
            dp = nt(v, g)
            dot = jnp.sum(low.astype(F32) * dp, axis=0, keepdims=True)
            ds = (prob * (dp - dot)).astype(BF16)
            kvg_v[:, vcols] = nn(low, g).astype(BF16)
            kvg_v[:, cols] = (nn(ds, q) * scale).astype(BF16)
            grad = (g.astype(F32) + tn(ds, k) * scale).astype(BF16)
            for i, col in enumerate(heads):
                ig_v[c, :, col] = grad[i * SPAN : (i + 1) * SPAN]

    def project(c):
        kvg = kvg_v[...]
        other = nt(kvg, w_v[1 - sec])
        for n in range(NB):
            xsend_v[c, n] = pack_half(other, n).astype(BF16)
        proj_copy(c).start()
        mine = nt(kvg, w_v[sec])
        for n in range(NB):
            own_v[c, n] = pack_half(mine, n)

    def step(t, carry):
        c = t - (1 - sec)
        live = (c >= 0) & (c < spans)

        @pl.when(live)
        def _():
            load(c, 0).wait()
            load(c, 1).wait()

            @pl.when(sec == 1)
            def _():
                load(c, 2).wait()

            @pl.when(sec == 0)
            def _():
                cot_copy(c).wait_recv()

            attend(c)
            out_copy(c).start()

            @pl.when(sec == 1)
            def _():
                cot_copy(c).start()

        s = t - LAG_SUM

        @pl.when((s >= 0) & (s < spans))
        def _():
            proj_copy(s).wait_recv()
            for n in range(NB):
                gown_v[s, n] = (own_v[s, n] + xrecv_v[s, n].astype(F32)).astype(BF16)
            for p in range(3):
                for way in range(2):
                    gather_copy(s, p, way).start()
            own_copy(s).start()

        f = t - LAG_FWD

        @pl.when((f >= 0) & (f < spans))
        def _():
            for p in range(3):
                for way in range(2):
                    gather_copy(f, p, way).wait_recv()
                    forward_copy(f, p, way).start()

        @pl.when(live)
        def _():
            project(c)

        return carry

    lax.fori_loop(0, spans + LAG_FWD, step, 0)

    def finish(c, carry):
        out_copy(c).wait()

        @pl.when(sec == 1)
        def _():
            cot_copy(c).wait_send()

        proj_copy(c).wait_send()
        own_copy(c).wait()
        for p in range(3):
            for way in range(2):
                gather_copy(c, p, way).wait_send()
                forward_copy(c, p, way).wait()
        return carry

    lax.fori_loop(0, spans, finish, 0)


def relay(queries, nb_kv, out_grad, weight):
    spans = nb_kv.shape[0]
    kvw2 = nb_kv.shape[-1]
    inner = queries.shape[-1]
    dma = pltpu.SemaphoreType.DMA
    item = (spans, NB, HALF, 128)
    any_spec = pl.BlockSpec(memory_space=pl.ANY)
    return pl.pallas_call(
        relay_kernel,
        name="relay",
        out_shape=(
            jax.ShapeDtypeStruct((spans, SPAN, inner), BF16),
            jax.ShapeDtypeStruct((RING,) + item, BF16),
        ),
        in_specs=[any_spec] * 4,
        out_specs=(any_spec, any_spec),
        scratch_shapes=[
            pltpu.VMEM((spans, SPAN, inner), BF16),
            pltpu.VMEM((spans, NB * NBLEN, kvw2), BF16),
            pltpu.VMEM((spans, SPAN, inner), BF16),
            pltpu.VMEM((spans, SPAN, inner), BF16),
            pltpu.VMEM((2, 512, kvw2), BF16),
            pltpu.VMEM((NB * NBLEN, kvw2), BF16),
            pltpu.VMEM(item, F32),
            pltpu.VMEM(item, BF16),
            pltpu.VMEM(item, BF16),
            pltpu.VMEM(item, BF16),
            dma((spans, 3)),
            dma((2, 2)),
            dma((spans,)),
            dma((spans,)),
            dma((spans,)),
            dma((spans,)),
            dma((spans,)),
            dma((spans,)),
            dma((spans, 3, 2)),
            dma((spans, 3, 2)),
            dma((spans, 3, 2)),
            dma((spans, 3, 2)),
        ],
        compiler_params=pltpu.CompilerParams(
            collective_id=0, has_side_effects=True, vmem_limit_bytes=48 * 2**20
        ),
        cost_estimate=pl.CostEstimate(flops=7 * 10**9, bytes_accessed=20 * 10**6, transcendentals=2**21),
    )(
        queries.reshape(spans, SPAN, inner),
        nb_kv.reshape(spans, NB * NBLEN, kvw2),
        out_grad.reshape(spans, SPAN, inner),
        weight,
    )


def route_kernel(cap, table, gath_hbm, out_ref, prefix, *refs):
    names = ("gath", "msend", "mrecv", "mtrans", "psend", "rtrans", "rrecv")
    buf = {name: refs[3 * i : 3 * i + 3] for i, name in enumerate(names)}
    (ld_sem, m_send, m_recv, mt_send, mt_recv, mf_send, mf_recv,
     rt_send, rt_recv, r0_send, r0_recv, r1_send, r1_recv) = refs[3 * len(names) :]
    total = RING * cap
    half = cap // 2
    near = neighbours()
    first, order, keep, last = 0, 3 * total, 6 * total, 9 * total

    def load(p):
        return pltpu.make_async_copy(gath_hbm.at[:, pl.ds(*PARTS[p])], buf["gath"][p], ld_sem.at[p])

    def remote(p, way, src, dst, send, recv):
        return pltpu.make_async_remote_copy(
            src, dst, send.at[p, way], recv.at[p, way], device_id=near[(p + 1) % 3][way], device_id_type=MESH
        )

    def remote3(p, way, src, dst, send, recv):
        return pltpu.make_async_remote_copy(
            src, dst, send.at[p, way], recv.at[p, way], device_id=near[(p + 2) % 3][way], device_id_type=MESH
        )

    def mid_direct(p, way):
        d = 1 + 2 * way
        return remote(p, way, buf["msend"][p].at[pl.ds((d - 1) * cap, cap)],
                      buf["mrecv"][p].at[pl.ds(d * cap, cap)], m_send, m_recv)

    def mid_transit(p, way):
        return remote(p, way, buf["msend"][p].at[pl.ds(cap + way * half, half)],
                      buf["mtrans"][p].at[way], mt_send, mt_recv)

    def mid_forward(p, way):
        return remote(p, way, buf["mtrans"][p].at[way],
                      buf["mrecv"][p].at[pl.ds(2 * cap + way * half, half)], mf_send, mf_recv)

    def far(p, way):
        return remote3(p, way, buf["psend"][p].at[pl.ds(32 + 8 * way, 8)], buf["rtrans"][p].at[way], rt_send, rt_recv)

    def near_now(p, way):
        d = 1 + 2 * way
        part = 8 * (1 - way)
        return remote3(p, way, buf["psend"][p].at[pl.ds(16 * d + part, 8)],
                       buf["rrecv"][p].at[way, pl.ds(part, 8)], r0_send, r0_recv)

    def near_late(p, way):
        d = 1 + 2 * way
        part = 8 * way
        return remote3(p, way, buf["psend"][p].at[pl.ds(16 * d + part, 8)],
                       buf["rrecv"][p].at[way, pl.ds(part, 8)], r1_send, r1_recv)

    for p in range(3):
        load(p).start()
    greet([d for pair in near for d in pair])
    prefix[total] = jnp.zeros(prefix.shape[1:], BF16)

    def fill(p, d):
        def body(j, carry):
            index = table[first + p * total + d * cap + j]
            value = buf["gath"][p][index]
            if d == 0:
                buf["mrecv"][p][j] = value
            else:
                buf["msend"][p][(d - 1) * cap + j] = value
            return carry

        lax.fori_loop(0, cap, body, 0)

    for p in range(3):
        load(p).wait()
        fill(p, 2)
        mid_transit(p, 0).start()
        mid_transit(p, 1).start()
    for p in range(3):
        fill(p, 1)
        mid_direct(p, 0).start()
        fill(p, 3)
        mid_direct(p, 1).start()
    for p in range(3):
        for way in range(2):
            mid_transit(p, way).wait_recv()
            mid_forward(p, way).start()
    for p in range(3):
        fill(p, 0)

    for p in range(3):
        size = PARTS[p][1]
        for way in range(2):
            mid_direct(p, way).wait_recv()
            mid_forward(p, way).wait_recv()

        def run(n, acc, p=p, size=size):
            value = buf["mrecv"][p][table[order + p * total + n]].astype(F32)
            acc = acc * table[keep + p * total + n].astype(F32) + value
            prefix[n, pl.ds(0, size)] = acc.astype(BF16)
            return acc

        lax.fori_loop(0, total, run, jnp.zeros((size, 128), F32))

        def rows(d, p=p, size=size):
            def body(r, carry):
                index = table[last + p * 64 + d * 16 + r]
                buf["psend"][p][d * 16 + r] = prefix[index, pl.ds(0, size)]
                return carry

            lax.fori_loop(0, ROWS_DEV, body, 0)

        rows(2)
        far(p, 0).start()
        far(p, 1).start()
        rows(1)
        near_now(p, 0).start()
        rows(3)
        near_now(p, 1).start()
        rows(0)

    for p in range(3):
        for way in range(2):
            far(p, way).wait_recv()
            base = 16 * (1 + 2 * way) + 8 * way

            def add(r, carry, p=p, way=way, base=base):
                buf["psend"][p][base + r] = (
                    buf["psend"][p][base + r].astype(F32) + buf["rtrans"][p][way, r].astype(F32)
                ).astype(BF16)
                return carry

            lax.fori_loop(0, 8, add, 0)
            near_late(p, way).start()
    for p in range(3):
        for way in range(2):
            near_now(p, way).wait_recv()
            near_late(p, way).wait_recv()

        def final(r, carry, p=p):
            out_ref[r, pl.ds(*PARTS[p])] = (
                buf["psend"][p][r].astype(F32)
                + buf["rrecv"][p][0, r].astype(F32)
                + buf["rrecv"][p][1, r].astype(F32)
            ).astype(BF16)
            return carry

        lax.fori_loop(0, ROWS_DEV, final, 0)
    for p in range(3):
        for way in range(2):
            mid_direct(p, way).wait_send()
            mid_transit(p, way).wait_send()
            mid_forward(p, way).wait_send()
            far(p, way).wait_send()
            near_now(p, way).wait_send()
            near_late(p, way).wait_send()


def route(cap, ident, gathered, table):
    items = gathered.shape[0]
    total = RING * cap
    sizes = [size for _, size in PARTS]
    dma = pltpu.SemaphoreType.DMA

    def per_part(*lead):
        return [pltpu.VMEM(lead + (size, 128), BF16) for size in sizes]

    return pl.pallas_call(
        functools.partial(route_kernel, cap),
        name="route%d" % cap,
        out_shape=jax.ShapeDtypeStruct((ROWS_DEV, HALF, 128), BF16),
        in_specs=[pl.BlockSpec(memory_space=pltpu.SMEM), pl.BlockSpec(memory_space=pl.ANY)],
        out_specs=pl.BlockSpec(memory_space=pltpu.VMEM),
        scratch_shapes=[pltpu.VMEM((total + 1, max(sizes), 128), BF16)]
        + per_part(items)
        + per_part(3 * cap)
        + per_part(total)
        + per_part(2, cap // 2)
        + per_part(64)
        + per_part(2, 8)
        + per_part(2, ROWS_DEV)
        + [dma((3,))]
        + [dma((3, 2))] * 12,
        compiler_params=pltpu.CompilerParams(
            collective_id=ident, has_side_effects=True, vmem_limit_bytes=60 * 2**20
        ),
        cost_estimate=pl.CostEstimate(flops=10**7, bytes_accessed=10**7, transcendentals=0),
    )(table, gathered)


def part_axes(p):
    return p, (p + 1) % 3, (p + 2) % 3


def plane_items(listing):
    me = lax.axis_index("ctx")
    coords = [(me // s) % RING for s in STRIDES]
    ring = jnp.arange(RING)
    picks = []
    for p in range(3):
        a1, a2, a3 = part_axes(p)
        one = jnp.mod(coords[a1] - ring, RING) * STRIDES[a1]
        two = jnp.mod(coords[a2] - ring, RING) * STRIDES[a2]
        picks.append(two[:, None] + one[None, :] + coords[a3] * STRIDES[a3])
    return listing[jnp.stack(picks)].reshape(3, RING, -1), coords


def owner_coords(codes):
    owner = codes // ROWS_DEV
    return [(owner // s) % RING for s in STRIDES]


def most_slots(listing):
    own = owner_coords(listing.reshape(RING, RING, RING, -1))
    most = 0
    classes = jnp.arange(RING * RING)
    for p in range(3):
        a1, a2, _ = part_axes(p)
        label = own[a1] * RING + own[a2]
        hits = (label[..., None] == classes).astype(jnp.int32)
        most = jnp.maximum(most, jnp.max(jnp.sum(hits, axis=(p, 3))))
    return most


def tables(listing, cap):
    total = RING * cap
    codes, coords = plane_items(listing)
    own = owner_coords(codes)
    axes = [part_axes(p) for p in range(3)]

    def along(which):
        values = jnp.stack([own[axes[p][which]][p] for p in range(3)])
        mine = jnp.stack([coords[axes[p][which]] for p in range(3)])
        return values, mine

    o1, m1 = along(0)
    o2, m2 = along(1)
    o3, m3 = along(2)
    entries = codes.shape[-1]
    entry = jnp.arange(entries)
    line_rel = o1[:, 0] == m1[:, None]
    line_d = jnp.mod(o2[:, 0] - m2[:, None], RING)
    earlier = entry[None, :] < entry[:, None]
    rank = jnp.sum(
        (line_rel[:, None, :] & (line_d[:, None, :] == line_d[:, :, None]) & earlier).astype(jnp.int32), axis=-1
    )
    slot = jnp.where(line_rel, line_d * cap + rank, -1)
    send = jnp.sum(jnp.where(slot[:, None, :] == jnp.arange(total)[None, :, None], entry, 0), axis=-1)
    rel = (o1 == m1[:, None, None]) & (o2 == m2[:, None, None])
    got = jnp.sum((rel[:, :, None, :] & earlier).astype(jnp.int32), axis=-1)
    place = (jnp.arange(RING)[None, :, None] * cap + got).reshape(3, -1)
    key = (jnp.mod(o3 - m3[:, None, None], RING) * ROWS_DEV + codes % ROWS_DEV).reshape(3, -1)
    rel = rel.reshape(3, -1)
    key = jnp.where(rel, key, 64)
    full = jnp.where(rel, key * total + place, 64 * total)
    pos = jnp.sum((full[:, None, :] < full[:, :, None]).astype(jnp.int32), axis=-1)
    follows = jnp.any((key[:, None, :] == key[:, :, None]) & (place[:, None, :] < place[:, :, None]), axis=-1)
    at = (pos[:, None, :] == jnp.arange(total)[None, :, None]) & rel[:, None, :]
    order = jnp.sum(jnp.where(at, place[:, None, :], 0), axis=-1)
    keep = jnp.sum(jnp.where(at, follows[:, None, :].astype(jnp.int32), 0), axis=-1)
    wanted = jnp.arange(64)[None, :, None]
    below = jnp.sum((key[:, None, :] <= wanted).astype(jnp.int32), axis=-1)
    exists = jnp.any(key[:, None, :] == wanted, axis=-1)
    last = jnp.where(exists, below - 1, total)
    return jnp.concatenate([send.reshape(-1), order.reshape(-1), keep.reshape(-1), last.reshape(-1)])


def local(queries, nb_kv, out_grad, kv_weight, nb_owner, nb_row):
    codes = (nb_owner * ROWS_DEV + nb_row).reshape(1, -1)
    listing = lax.all_gather(codes, "ctx", axis=0, tiled=True)
    input_grad, gathered = relay(queries[0], nb_kv[0], out_grad, kv_weight[0])
    gathered = gathered.reshape(-1, HALF, 128)
    worst = RING * RING * CAP
    few = worst // 2
    fits = most_slots(listing) <= few
    packed = lax.cond(
        fits,
        lambda g: route(few, 1, g, tables(listing, few)),
        lambda g: route(worst, 2, g, tables(listing, worst)),
        gathered,
    )
    wide = packed[:, :384].reshape(ROWS_DEV, 3, NBLEN, 128).transpose(0, 2, 1, 3).reshape(ROWS_DEV, NBLEN, 384)
    tail = packed[:, 384:].reshape(ROWS_DEV, 64, 2, 64).transpose(0, 2, 1, 3).reshape(ROWS_DEV, NBLEN, 64)
    enc = jnp.concatenate([wide, tail], axis=-1)
    return (input_grad.reshape(queries.shape), enc)


def solution(mesh):
    in_specs = (
        P("section", "ctx", None),
        P("section", "ctx", None, None, None),
        P("ctx", None),
        P("section", None, None),
        P("ctx", None),
        P("ctx", None),
    )
    out_specs = (P("section", "ctx", None), P("ctx", None, "section"))
    return jax.shard_map(local, mesh=mesh, in_specs=in_specs, out_specs=out_specs, check_vma=False)
```

time: 1430 us -> 306 us (0.21)
  blocking collectives: 938 us -> 177 us
  local copies, waits for them, and re-layouts: 236 us -> 15.5 us
  matrix products: 109 us -> 0 us
  Pallas kernels: 0 us -> 99.8 us
  other arithmetic: 96.2 us -> 9.92 us
    all_gather x2 -> x1, blocking collectives: 938 us -> 177 us  [local(): listing = lax.all_gather(codes, 'ctx', axis=0, tiled=True)]
    dot_general x27 -> x0, matrix products: 109 us -> none  [the longest x1 19.8 us: local(): lax.dot_general(summed.reshape(item_count * token_count, -1), weight_wide...]
    pallas_call x0 -> x2, Pallas kernels: none -> 99.8 us  [the longest x1 61.2 us: route(): pl.pallas_call(functools.partial(route_kernel, cap), name='route%d' % cap...]
    dot_general x2 -> x0, local copies, waits for them, and re-layouts: 74.6 us -> none  [the longest x1 43.9 us: local(): jnp.dot(recv_table, received_slots.reshape(slot_count, -1), preferred_ele...]
    sub x4 -> x0, other arithmetic: 44.5 us -> none  [span_backward(): weights_raw = jnp.exp(scores - row_peak)]
    reshape x21 -> x9, local copies, waits for them, and re-layouts: 47.1 us -> 5.46 us  [the longest x1 2.58 us: local(): packed[:, :384].reshape(ROWS_DEV, 3, NBLEN, 128).transpose(0, 2, 1, 3)]
    dynamic_update_slice x8 -> x0, other arithmetic: 30.5 us -> none  [run_block(): lax.map(group_backward, (query_groups, grad_groups, kv_groups))]
    unnamed x10 -> x6, local copies, waits for them, and re-layouts: 30.9 us -> 4.49 us
  transfers between devices with their start and end apart: 3 -> 0, of which waited for: 2 -> 0; matrix products, arithmetic and copies ran while one was open for 0% -> 0% of each run, Pallas kernels for 0% -> 0%
where the time goes in v1:
time: 306 us; the launch traced here: 305 us
  blocking collectives  177 us (58%)
  Pallas kernels  99.8 us (33%)
  local copies, waits for them, and re-layouts  15.5 us (5%)
  other arithmetic  9.92 us (3%)
    all_gather x1, blocking collectives, local(): listing = lax.all_gather(codes, 'ctx', axis=0, tiled=True)  177 us
    pallas_call x1, Pallas kernels, route(): pl.pallas_call(functools.partial(route_kernel, cap), name='route%d' % cap...  61.2 us
    pallas_call x1, Pallas kernels, relay(): pl.pallas_call(relay_kernel, name='relay', out_shape=(jax.ShapeDtypeStruc...  38.6 us

profile of v1, /device:TPU:0, one launch (start us, length us, event | category | flops | bytes accessed | tf_op | source)
XLA Modules:
  0.0 305.2 jit_solution(35643667512084214)
XLA Ops:
  0.6 0.7 multiply_add_fusion.3
  1.3 0.1 copy.27
  1.4 0.1 reshape.2652
  1.5 177.2 %all-gather = s32[64,1,16]{2,1,0:T(1,128)S(1)} all-gather(s32[1,1,16]{2,1,0:T(1,128)S(1)} %reshape.2652), channel_id=1, replica_groups=mesh['section'=2,'ctx'=64] {'ctx'}, dimensions={0}, use_global_device_ids=true | all-gather | bytes 4160 | tf_op jit(solution)/shard_map/all_gather | solution.py:569
  178.7 0.1 multiply_add_fusion
  178.8 0.2 convert_reduce_fusion.8
  179.0 0.7 reduce_max.29
  179.7 0.1 multiply_add_fusion.1
  179.8 0.2 convert_reduce_fusion.9
  180.1 0.6 reduce_max.28
  180.8 0.2 convert_reduce_fusion.10
  181.0 0.6 reduce_max.27
  183.6 1.6 copy-done
  185.2 1.5 copy-done.1
  186.7 38.6 %relay.1 = (bf16[8,64,2048]{2,1,0:T(8,128)(2,1)S(1)}, bf16[4,8,2,448,128]{4,3,2,1,0:T(8,128)(2,1)}) custom-call(bf16[8,64,2048]{2,1,0:T(8,128)(2,1)S(1)} %bitcast.77, bf16[8,256,1024]{2,1,0:T(8,128)(2,1)} %bitcast.90, bf16[8,64,2048]{2,1,0:T(8,128)(2,1)} %bitcast.91, bf16[896,1024]{1,0:T(8,128)(2,1)S(1)} %bitcast.78), custom_call_target="tpu_custom_call" | custom-call | flops 7000000000 | bytes 20000000 | tf_op jit(solution)/shard_map/relay/pallas_call | solution.py:260
  225.3 67.0 %conditional.1 = (bf16[16,448,128]{2,1,0:T(8,128)(2,1)}) conditional(s32[]{:T(128)} %convert_element_type.55, (s32[64,16]{1,0:T(8,128)S(1)}, bf16[64,448,128]{2,1,0:T(8,128)(2,1)}) %tuple.76, (s32[64,16]{1,0:T(8,128)S(1)}, bf16[64,448,128]{2,1,0:T(8,128)(2,1)}) %tuple.77), branch_computations={%region_6.16_spmd, %region_16.26_spmd} | conditional | flops 12605173 | bytes 10221628 | solution.py:575
  225.7 0.1 add.813
  225.8 0.1 reshape.2640
  225.9 0.6 gather_fusion.1
  226.5 0.1 reshape.2609
  226.8 0.1 stack.129
  227.1 0.1 stack.131
  227.2 0.1 stack.122
  227.3 0.1 stack.125
  227.4 0.1 stack.127
  227.4 0.1 stack.121
  228.0 0.2 convert_reduce_fusion.7
  228.3 0.3 convert_reduce_fusion.5
  228.6 0.1 reduce_sum.153
  228.6 0.1 add_select_fusion.20
  228.7 0.3 convert_reduce_fusion.4
  229.0 0.1 select_reduce_fusion.5
  229.2 0.1 reshape.2608
  229.3 0.2 fusion.25
  229.4 0.4 and_reduce_fusion.1
  229.9 0.1 convert_reduce_fusion.6
  230.0 0.1 select_n.466
  230.1 0.2 select_reduce_fusion.4
  230.5 0.7 pad_add_fusion.8.table
  231.2 61.2 %route16.1 = bf16[16,448,128]{2,1,0:T(8,128)(2,1)} custom-call(s32[768]{0:T(1024)} %pad_add_fusion.8.table, bf16[64,448,128]{2,1,0:T(8,128)(2,1)} %get-tuple-element.14.gath_hbm), custom_call_target="tpu_custom_call" | custom-call | flops 10000000 | bytes 10000000 | tf_op jit(solution)/shard_map/cond/branch_1_fun/route16/pallas_call | solution.py:467
  292.4 1.0 slice.73
  293.3 2.7 slice.72
  296.0 2.6 copy.28
  298.6 0.2 reshape.2628
  298.9 2.0 copy.29
  300.9 0.2 reshape.2629
  301.1 2.8 pad_maximum_fusion
  303.9 1.3 copy.65
  (34 shorter events, 1.5 us)
Async XLA Ops:
  183.6 1.6 copy-start
  185.2 1.5 copy-start.1

commit v2 on v1

--- a/solution.py
+++ b/solution.py
@@ -59,23 +59,11 @@
     return lax.dot_general(a, b, (((0,), (0,)), ((), ())), preferred_element_type=F32)
 
 
-def pack_half(prod, n):
-    base = n * NBLEN
-    blocks = [prod[base : base + NBLEN, j * 128 : (j + 1) * 128] for j in range(3)]
-    lane = lax.broadcasted_iota(jnp.int32, (NBLEN // 2, 128), 1)
-    tail = jnp.where(
-        lane < 64,
-        prod[base : base + NBLEN // 2, 384:512],
-        prod[base + NBLEN // 2 : base + NBLEN, 384:512],
-    )
-    return jnp.concatenate(blocks + [tail], axis=0)
-
-
 def relay_kernel(
-    q_hbm, kv_hbm, og_hbm, w_hbm, ig_hbm, gath_hbm,
+    q_hbm, kv_hbm, og_hbm, w_hbm, code_hbm, ig_hbm, gath_hbm, list_hbm,
     q_v, kv_v, cot_v, ig_v, w_v, kvg_v, own_v, xsend_v, xrecv_v, gown_v,
     ld_sem, w_sem, out_sem, cs_send, cs_recv, xs_send, xs_recv, gl_sem,
-    ag_send, ag_recv, fw_send, fw_recv,
+    ag_send, ag_recv, fw_send, fw_recv, ls_sem, ls_send, ls_recv,
 ):
     spans = kv_v.shape[0]
     sec = lax.axis_index("section")
@@ -88,12 +76,19 @@
         hbm, vmem = ((q_hbm, q_v), (kv_hbm, kv_v), (og_hbm, cot_v))[which]
         return pltpu.make_async_copy(hbm.at[c], vmem.at[c], ld_sem.at[c, which])
 
-    def load_w(half, piece):
-        if piece == 0:
-            source, target = pl.ds(half * HALF, HALF), pl.ds(0, HALF)
-        else:
-            source, target = pl.ds(half * HALF + 384, 64), pl.ds(HALF, 64)
-        return pltpu.make_async_copy(w_hbm.at[source], w_v.at[half, target], w_sem.at[half, piece])
+    def load_w():
+        return pltpu.make_async_copy(w_hbm, w_v, w_sem)
+
+    def list_own():
+        return pltpu.make_async_copy(code_hbm, list_hbm.at[0, 0, 0], ls_sem)
+
+    def list_copy(stage, hop):
+        view = (lambda k: list_hbm.at[0, 0, k], lambda k: list_hbm.at[0, k], lambda k: list_hbm.at[k])[stage]
+        source, target = ((0, 1), (0, 3), (1, 2))[hop]
+        return pltpu.make_async_remote_copy(
+            view(source), view(target), ls_send.at[stage, hop], ls_recv.at[stage, hop],
+            device_id=near[2 - stage][hop % 2], device_id_type=MESH,
+        )
 
     def out_copy(c):
         return pltpu.make_async_copy(ig_v.at[c], ig_hbm.at[c], out_sem.at[c])
@@ -136,16 +131,16 @@
         return carry
 
     lax.fori_loop(0, 1, start_loads, 0)
-    for half in range(2):
-        for piece in range(2):
-            load_w(half, piece).start()
+    load_w().start()
+    list_own().start()
     lax.fori_loop(1, spans, start_loads, 0)
 
     greet([partner] + [d for pair in near for d in pair])
 
-    for half in range(2):
-        for piece in range(2):
-            load_w(half, piece).wait()
+    list_own().wait()
+    list_copy(0, 0).start()
+    list_copy(0, 1).start()
+    load_w().wait()
 
     def attend(c):
         for h in range(KV_HEADS):
@@ -171,13 +166,29 @@
 
     def project(c):
         kvg = kvg_v[...]
-        other = nt(kvg, w_v[1 - sec])
+        other = nt(w_v[1 - sec], kvg)
         for n in range(NB):
-            xsend_v[c, n] = pack_half(other, n).astype(BF16)
+            xsend_v[c, n] = other[:, n * NBLEN : (n + 1) * NBLEN].astype(BF16)
         proj_copy(c).start()
-        mine = nt(kvg, w_v[sec])
+        mine = nt(w_v[sec], kvg)
         for n in range(NB):
-            own_v[c, n] = pack_half(mine, n)
+            own_v[c, n] = mine[:, n * NBLEN : (n + 1) * NBLEN]
+
+    def spread_lists(t):
+        for stage in range(3):
+
+            @pl.when(t == 2 * stage + 1)
+            def _(stage=stage):
+                list_copy(stage, 0).wait_recv()
+                list_copy(stage, 2).start()
+
+            @pl.when(t == 2 * stage + 2)
+            def _(stage=stage):
+                list_copy(stage, 1).wait_recv()
+                list_copy(stage, 2).wait_recv()
+                if stage < 2:
+                    list_copy(stage + 1, 0).start()
+                    list_copy(stage + 1, 1).start()
 
     def step(t, carry):
         c = t - (1 - sec)
@@ -203,6 +214,7 @@
             def _():
                 cot_copy(c).start()
 
+        spread_lists(t)
         s = t - LAG_SUM
 
         @pl.when((s >= 0) & (s < spans))
@@ -248,9 +260,12 @@
         return carry
 
     lax.fori_loop(0, spans, finish, 0)
-
-
-def relay(queries, nb_kv, out_grad, weight):
+    for stage in range(3):
+        for hop in range(3):
+            list_copy(stage, hop).wait_send()
+
+
+def relay(queries, nb_kv, out_grad, weight, codes):
     spans = nb_kv.shape[0]
     kvw2 = nb_kv.shape[-1]
     inner = queries.shape[-1]
@@ -263,22 +278,23 @@
         out_shape=(
             jax.ShapeDtypeStruct((spans, SPAN, inner), BF16),
             jax.ShapeDtypeStruct((RING,) + item, BF16),
+            jax.ShapeDtypeStruct((RING, RING, RING, 1, 128), jnp.int32),
         ),
-        in_specs=[any_spec] * 4,
-        out_specs=(any_spec, any_spec),
+        in_specs=[any_spec] * 5,
+        out_specs=(any_spec,) * 3,
         scratch_shapes=[
             pltpu.VMEM((spans, SPAN, inner), BF16),
             pltpu.VMEM((spans, NB * NBLEN, kvw2), BF16),
             pltpu.VMEM((spans, SPAN, inner), BF16),
             pltpu.VMEM((spans, SPAN, inner), BF16),
-            pltpu.VMEM((2, 512, kvw2), BF16),
+            pltpu.VMEM((2, HALF, kvw2), BF16),
             pltpu.VMEM((NB * NBLEN, kvw2), BF16),
             pltpu.VMEM(item, F32),
             pltpu.VMEM(item, BF16),
             pltpu.VMEM(item, BF16),
             pltpu.VMEM(item, BF16),
             dma((spans, 3)),
-            dma((2, 2)),
+            dma(()),
             dma((spans,)),
             dma((spans,)),
             dma((spans,)),
@@ -289,16 +305,20 @@
             dma((spans, 3, 2)),
             dma((spans, 3, 2)),
             dma((spans, 3, 2)),
+            dma(()),
+            dma((3, 3)),
+            dma((3, 3)),
         ],
         compiler_params=pltpu.CompilerParams(
-            collective_id=0, has_side_effects=True, vmem_limit_bytes=48 * 2**20
+            collective_id=0, has_side_effects=True, vmem_limit_bytes=60 * 2**20
         ),
         cost_estimate=pl.CostEstimate(flops=7 * 10**9, bytes_accessed=20 * 10**6, transcendentals=2**21),
     )(
         queries.reshape(spans, SPAN, inner),
         nb_kv.reshape(spans, NB * NBLEN, kvw2),
         out_grad.reshape(spans, SPAN, inner),
-        weight,
+        weight.reshape(2, HALF, kvw2),
+        codes,
     )
 
 
@@ -494,14 +514,8 @@
 def plane_items(listing):
     me = lax.axis_index("ctx")
     coords = [(me // s) % RING for s in STRIDES]
-    ring = jnp.arange(RING)
-    picks = []
-    for p in range(3):
-        a1, a2, a3 = part_axes(p)
-        one = jnp.mod(coords[a1] - ring, RING) * STRIDES[a1]
-        two = jnp.mod(coords[a2] - ring, RING) * STRIDES[a2]
-        picks.append(two[:, None] + one[None, :] + coords[a3] * STRIDES[a3])
-    return listing[jnp.stack(picks)].reshape(3, RING, -1), coords
+    planes = [listing[:, :, 0].swapaxes(0, 1), listing[0].swapaxes(0, 1), listing[:, 0]]
+    return jnp.stack(planes).reshape(3, RING, -1), coords
 
 
 def owner_coords(codes):
@@ -510,7 +524,7 @@
 
 
 def most_slots(listing):
-    own = owner_coords(listing.reshape(RING, RING, RING, -1))
+    own = owner_coords(listing)
     most = 0
     classes = jnp.arange(RING * RING)
     for p in range(3):
@@ -566,8 +580,10 @@
 
 def local(queries, nb_kv, out_grad, kv_weight, nb_owner, nb_row):
     codes = (nb_owner * ROWS_DEV + nb_row).reshape(1, -1)
-    listing = lax.all_gather(codes, "ctx", axis=0, tiled=True)
-    input_grad, gathered = relay(queries[0], nb_kv[0], out_grad, kv_weight[0])
+    entries = codes.shape[-1]
+    codes = jnp.pad(codes, ((0, 0), (0, 128 - entries)))
+    input_grad, gathered, listing = relay(queries[0], nb_kv[0], out_grad, kv_weight[0], codes)
+    listing = listing[..., 0, :entries]
     gathered = gathered.reshape(-1, HALF, 128)
     worst = RING * RING * CAP
     few = worst // 2
@@ -578,10 +594,7 @@
         lambda g: route(worst, 2, g, tables(listing, worst)),
         gathered,
     )
-    wide = packed[:, :384].reshape(ROWS_DEV, 3, NBLEN, 128).transpose(0, 2, 1, 3).reshape(ROWS_DEV, NBLEN, 384)
-    tail = packed[:, 384:].reshape(ROWS_DEV, 64, 2, 64).transpose(0, 2, 1, 3).reshape(ROWS_DEV, NBLEN, 64)
-    enc = jnp.concatenate([wide, tail], axis=-1)
-    return (input_grad.reshape(queries.shape), enc)
+    return (input_grad.reshape(queries.shape), packed.swapaxes(1, 2))
 
 
 def solution(mesh):

time: 306 us -> 123 us (0.40)
  blocking collectives: 177 us -> 0 us
  local copies, waits for them, and re-layouts: 15.5 us -> 7.02 us
  Pallas kernels: 99.8 us -> 106 us
    all_gather x1 -> x0, blocking collectives: 177 us -> none  [local(): listing = lax.all_gather(codes, 'ctx', axis=0, tiled=True)]
    pallas_call x1, Pallas kernels: 38.6 us -> 47 us  [relay(): pl.pallas_call(relay_kernel, name='relay', out_shape=(jax.ShapeDtypeStruc...]
    reshape x6 -> x1, local copies, waits for them, and re-layouts: 5.21 us -> 0.08 us  [local(): codes = (nb_owner * ROWS_DEV + nb_row).reshape(1, -1)]
    slice x2 -> x1, local copies, waits for them, and re-layouts: 3.68 us -> 0.03 us  [plane_items(): listing[:, 0]]
where the time goes in v2:
time: 123 us
  Pallas kernels  106 us (86%)
  local copies, waits for them, and re-layouts  7.02 us (6%)
  other arithmetic  6.99 us (6%)
  between operations  2.59 us (2%)
    pallas_call x1, Pallas kernels, route(): pl.pallas_call(functools.partial(route_kernel, cap), name='route%d' % cap...  59.1 us
    pallas_call x1, Pallas kernels, relay(): pl.pallas_call(relay_kernel, name='relay', out_shape=(jax.ShapeDtypeStruc...  47 us
    unnamed x2, local copies, waits for them, and re-layouts  4.39 us

profile of v2, /device:TPU:0, one launch (start us, length us, event | category | flops | bytes accessed | tf_op | source)
XLA Modules:
  0.0 122.9 jit_solution(14863007237722560637)
XLA Ops:
  0.6 0.7 multiply_add_fusion.3
  1.3 0.1 copy.26
  1.4 0.1 reshape.1987
  1.5 0.5 pad.4.code_hbm
  2.0 47.0 %relay.1 = (bf16[8,64,2048]{2,1,0:T(8,128)(2,1)}, bf16[4,8,2,448,128]{4,3,2,1,0:T(8,128)(2,1)}, s32[4,4,4,1,128]{4,3,2,1,0:T(1,128)S(1)}) custom-call(bf16[8,64,2048]{2,1,0:T(8,128)(2,1)} %bitcast.93, bf16[8,256,1024]{2,1,0:T(8,128)(2,1)} %bitcast.92, bf16[8,64,2048]{2,1,0:T(8,128)(2,1)} %bitcast.94, bf16[2,448,1024]{2,1,0:T(8,128)(2,1)} %bitcast.95, ...), custom_call_target="tpu_custom_call" | custom-call | flops 7000000000 | bytes 20000000 | tf_op jit(solution)/shard_map/relay/pallas_call | solution.py:275
  49.1 0.1 multiply_add_fusion
  49.2 0.2 convert_reduce_fusion.8
  49.4 0.7 reduce_max.29
  50.1 0.1 multiply_add_fusion.1
  50.2 0.2 convert_reduce_fusion.9
  50.4 0.6 reduce_max.28
  51.1 0.2 convert_reduce_fusion.10
  51.4 0.6 reduce_max.27
  53.9 64.5 %conditional.1 = (bf16[16,448,128]{2,1,0:T(8,128)(2,1)S(1)}) conditional(s32[]{:T(128)} %convert_element_type.55, (s32[4,4,4,16]{3,2,1,0:T(4,128)S(1)}, bf16[64,448,128]{2,1,0:T(8,128)(2,1)}) %tuple.78, (s32[4,4,4,16]{3,2,1,0:T(4,128)S(1)}, bf16[64,448,128]{2,1,0:T(8,128)(2,1)}) %tuple.79), branch_computations={%region_6.16_spmd, %region_16.26_spmd} | conditional | flops 12606731 | bytes 10227308 | solution.py:591
  54.3 0.1 add.365
  54.4 0.1 stack.145
  54.5 0.1 stack.121
  54.6 0.1 stack.146
  54.7 0.1 stack.144
  54.8 0.1 stack.120
  54.9 0.1 stack.122
  55.1 0.1 stack.139
  55.1 0.1 stack.133
  55.2 0.1 stack.136
  55.4 0.1 stack.141
  55.4 0.1 stack.132
  55.5 0.1 stack.135
  55.6 0.1 stack.137
  55.7 0.1 stack.131
  55.8 0.1 stack.140
  56.2 0.2 convert_reduce_fusion.7
  56.4 0.1 fusion.34
  56.5 0.3 convert_reduce_fusion.5
  56.8 0.1 reduce_sum.153
  56.9 0.1 add_select_fusion.20
  57.0 0.3 convert_reduce_fusion.4
  57.3 0.1 select_reduce_fusion.5
  57.4 0.1 reshape.1979
  57.5 0.2 fusion.19
  57.7 0.4 and_reduce_fusion.1
  58.1 0.1 convert_reduce_fusion.6
  58.3 0.1 select_n.360
  58.4 0.2 select_reduce_fusion.4
  58.6 0.1 reshape.1980
  58.7 0.7 pad_add_fusion.10.table
  59.4 59.1 %route16.1 = bf16[16,448,128]{2,1,0:T(8,128)(2,1)S(1)} custom-call(s32[768]{0:T(1024)} %pad_add_fusion.10.table, bf16[64,448,128]{2,1,0:T(8,128)(2,1)} %get-tuple-element.14.gath_hbm), custom_call_target="tpu_custom_call" | custom-call | flops 10000000 | bytes 10000000 | tf_op jit(solution)/shard_map/cond/branch_1_fun/route16/pallas_call | solution.py:487
  118.5 3.2 %copy.33 = bf16[1,512,2048]{2,1,0:T(8,128)(2,1)} copy(bf16[1,512,2048]{2,1,0:T(8,128)(2,1)} %bitcast.79) | data formatting | bytes 4194304
  121.6 1.2 copy.34
  (25 shorter events, 1.0 us)

commit v3 on v2

v3 whole, which is shorter than its diff:
```python
import functools
import math

import jax
import jax.numpy as jnp
from jax import lax
from jax.experimental import pallas as pl
from jax.experimental.pallas import tpu as pltpu
from jax.sharding import PartitionSpec as P

HEADS = 16
KV_HEADS = 4
GROUP = HEADS // KV_HEADS
HDIM = 128
SPAN = 64
NB = 2
NBLEN = 128
CAP = 2
RING = 4
ROWS_DEV = 16
STRIDES = (16, 4, 1)
HALF = 448
PARTS = ((0, 160), (160, 144), (304, 144))
PIECES = ((0, 0, 80), (1, 160, 80), (2, 304, 80), (0, 80, 80), (1, 240, 64), (2, 384, 64))
FAST = (16, 16, 8)
FULL = (RING * RING * CAP,) * 3
LAG_SUM = 2
LAG_FWD = 4
SHIFTS = (4, 2, 0)
F32 = jnp.float32
BF16 = jnp.bfloat16
MESH = pl.DeviceIdType.MESH


def axis_step(axis, delta):
    me = lax.axis_index("ctx")
    stride = STRIDES[axis]
    coord = lax.rem(me // stride, RING)
    return me + (lax.rem(coord + delta + RING, RING) - coord) * stride


def greet(devices):
    barrier = pltpu.get_barrier_semaphore()
    for device in devices:
        pl.semaphore_signal(barrier, inc=1, device_id=device, device_id_type=MESH)
    pl.semaphore_wait(barrier, len(devices))


def neighbours():
    sec = lax.axis_index("section")
    return [[(sec, axis_step(a, 1)), (sec, axis_step(a, -1))] for a in range(3)]


def nt(a, b):
    return lax.dot_general(a, b, (((1,), (1,)), ((), ())), preferred_element_type=F32)


def nn(a, b):
    return lax.dot_general(a, b, (((1,), (0,)), ((), ())), preferred_element_type=F32)


def tn(a, b):
    return lax.dot_general(a, b, (((0,), (0,)), ((), ())), preferred_element_type=F32)


def part_axes(p):
    return p, (p + 1) % 3, (p + 2) % 3


def flags(mask):
    return jnp.where(mask, 1.0, 0.0).astype(BF16)


def count(mask, axis):
    return jnp.sum(jnp.where(mask, 1, 0), axis=axis, keepdims=True)


def pick(mask, values):
    return jnp.sum(jnp.where(mask, values, 0), axis=0, keepdims=True)


def plan(list_v, table_ref, most_ref):
    me = lax.axis_index("ctx")
    coords = [lax.rem(me // s, RING) for s in STRIDES]
    codes = jnp.concatenate([list_v[:, 0, :], list_v[:, 1, :]], axis=0)
    owners = (codes >> 4).astype(F32).astype(BF16)
    places = (codes & 15).astype(F32).astype(BF16)

    def as_column(values, at_row, at_lane):
        lane = lax.broadcasted_iota(jnp.int32, (at_row.shape[0], 128), 1)
        rows = nn(flags(lane == at_row), values)
        return jnp.sum(jnp.where(lane == at_lane, rows, 0.0), axis=1, keepdims=True).astype(jnp.int32)

    def as_row(values, at_row, at_lane):
        sub = lax.broadcasted_iota(jnp.int32, (128, at_row.shape[1]), 0)
        columns = nn(values, flags(sub == at_lane))
        return jnp.sum(jnp.where(sub == at_row, columns, 0.0), axis=0, keepdims=True).astype(jnp.int32)

    def share(n1, n2, n3, cap):
        low, high = jnp.maximum(n2 + n3 - cap[1], 0), jnp.minimum(n2, cap[1] - n1)
        return jnp.minimum(jnp.maximum(n2 >> 1, low), high), low, high

    every = lax.broadcasted_iota(jnp.int32, (1, 1024), 1)
    device = every >> 4
    owner_all = as_row(owners, ((every >> 3) & 1) * 64 + device, every & 7)
    sub = lax.broadcasted_iota(jnp.int32, (32, 1024), 0)
    over = jnp.zeros((1, 1), jnp.int32)
    for p in range(3):
        a1, a2, a3 = part_axes(p)
        f1, f2, f3 = [SHIFTS[a] for a in (a1, a2, a3)]
        away = (((owner_all >> f2) & 3) - coords[a2] + ((device >> f2) & 3)) & 3
        label = away * 8 + ((owner_all >> f1) & 3)
        line = ((device >> f2) & 3) * 4 + ((device >> f3) & 3)
        hits = nt(flags(sub == label), flags(sub[0:16] == line)).astype(jnp.int32)
        n0, n1, n2, n3 = [hits[8 * d : 8 * d + 8] for d in range(4)]
        right, low, high = share(n1, n2, n3, FAST)
        bad = (n0 > FAST[0]) | (low > high) | (right > FAST[2]) | (n2 - right > FAST[2])
        bad = jnp.max(jnp.where(bad, 1, 0), axis=1, keepdims=True)
        over = jnp.maximum(over, jnp.max(bad, axis=0, keepdims=True))
    most_ref[0, 0] = jnp.max(over)

    number = lax.broadcasted_iota(jnp.int32, (1, 128), 1)
    col = lax.broadcasted_iota(jnp.int32, (256, 1), 0)
    row = lax.broadcasted_iota(jnp.int32, (1, 256), 1)
    same = row >> 6 == col >> 6
    item_c = (col & 48) | ((col & 7) * 2 + ((col >> 3) & 1))
    for p in range(3):
        a1, a2, a3 = part_axes(p)

        def both(values):
            found = []
            for e, form in ((col, as_column), (row, as_row)):
                at_row = ((e >> 3) & 1) * 64 + (e >> 6) * STRIDES[a2] + ((e >> 4) & 3) * STRIDES[a1]
                found.append(form(values, at_row, e & 7))
            return found

        (own_c, own_r), (place_c, place_r) = both(owners), both(places)

        def fields(own, spot, e):
            o1, o2, o3 = [(own >> SHIFTS[a]) & 3 for a in (a1, a2, a3)]
            away = jnp.where(o1 == coords[a1], (o2 - coords[a2] + (e >> 6)) & 3, RING)
            key = jnp.where(away == e >> 6, ((o3 - coords[a3]) & 3) * ROWS_DEV + spot, 64)
            return away, key

        away_c, key_c = fields(own_c, place_c, col)
        away_r, key_r = fields(own_r, place_r, row)
        rank_c = count(same & (away_r == away_c) & (row < col), 1)
        rank_r = count(same & (away_r == away_c) & (col < row), 0)
        many_c = [count(same & (away_r == d), 1) for d in (1, 2, 3)]
        many_r = [count(same & (away_c == d), 0) for d in (1, 2, 3)]
        below = count(key_c <= number, 0)
        present = count(key_c == number, 0)
        for which, cap in enumerate((FAST, FULL)):
            stay, slots, passed = cap
            base = which * 12 + p * 4

            def slot(away, rank, many, behind):
                right = share(*many, cap)[0]
                one = stay + right + rank
                three = stay + slots + many[1] - right + rank
                two = jnp.where(rank < right, behind[0] + rank, behind[1] + rank - right)
                return jnp.where(
                    away == 0, rank, jnp.where(away == 1, one, jnp.where(away == 2, two, three))
                )

            sent_c = jnp.where((away_c < RING) & (col < 64), slot(away_c, rank_c, many_c, (stay, stay + slots)), -1)
            table_ref[pl.ds(base, 1)] = pick(sent_c == number, item_c)
            far = (stay + 2 * slots, stay + 2 * slots + passed)
            spot_c = slot(away_c, rank_c, many_c, far)
            spot_r = slot(away_r, rank_r, many_r, far)
            full_c = key_c * 256 + spot_c
            full_r = key_r * 256 + spot_r
            ahead = (full_r < full_c) & (key_r < 64)
            pos_c = jnp.where(key_c < 64, count(ahead, 1), -1)
            follows_c = jnp.where(count(ahead & (key_r == key_c), 1) > 0, 1, 0)
            table_ref[pl.ds(base + 1, 1)] = pick(pos_c == number, spot_c)
            table_ref[pl.ds(base + 2, 1)] = pick(pos_c == number, follows_c)
            table_ref[pl.ds(base + 3, 1)] = jnp.where(present > 0, below - 1, RING * stay)


def relay_kernel(
    q_hbm, kv_hbm, og_hbm, w_hbm, owner_ref, row_ref, ig_hbm, gath_hbm, table_ref, most_ref,
    q_v, kv_v, cot_v, ig_v, w_v, kvg_v, xsend_v, xrecv_v, gown_v, list_v,
    ld_sem, w_sem, out_sem, cs_send, cot_sem, xs_send, xs_recv, gl_sem,
    ag_send, ag_recv, fw_send, fw_recv, ls_send, ls_recv,
):
    spans = kv_v.shape[0]
    sec = lax.axis_index("section")
    me = lax.axis_index("ctx")
    partner = (1 - sec, me)
    near = neighbours()
    scale = 1.0 / math.sqrt(HDIM)

    def load(c, which):
        hbm, vmem = ((q_hbm, q_v), (kv_hbm, kv_v))[which]
        return pltpu.make_async_copy(hbm.at[c], vmem.at[c], ld_sem.at[c, which])

    def cot_load(c):
        return pltpu.make_async_copy(og_hbm.at[c], cot_v.at[0, c], cot_sem.at[0, c])

    def cot_send(c):
        return pltpu.make_async_remote_copy(
            ig_v.at[c], cot_v.at[1 - sec, c], cs_send.at[c], cot_sem.at[1 - sec, c],
            device_id=partner, device_id_type=MESH,
        )

    def load_w():
        return pltpu.make_async_copy(w_hbm, w_v, w_sem)

    def list_copy(stage, hop):
        size = RING**stage
        source, target = ((0, 1), (0, 3), (1, 2))[hop]
        return pltpu.make_async_remote_copy(
            list_v.at[pl.ds(source * size, size)], list_v.at[pl.ds(target * size, size)],
            ls_send.at[stage, hop], ls_recv.at[stage, hop],
            device_id=near[2 - stage][hop % 2], device_id_type=MESH,
        )

    def out_copy(c):
        return pltpu.make_async_copy(ig_v.at[c], ig_hbm.at[c], out_sem.at[c])

    def proj_copy(c):
        return pltpu.make_async_remote_copy(
            xsend_v.at[c], xrecv_v.at[c], xs_send.at[c], xs_recv.at[c], device_id=partner, device_id_type=MESH
        )

    def own_copy(c):
        return pltpu.make_async_copy(gown_v.at[c], gath_hbm.at[0, c], gl_sem.at[c])

    def gather_copy(c, p, way):
        rows = pl.ds(*PARTS[p])
        return pltpu.make_async_remote_copy(
            gown_v.at[c, :, rows], gath_hbm.at[1 + 2 * way, c, :, rows],
            ag_send.at[c, p, way], ag_recv.at[c, p, way], device_id=near[p][way], device_id_type=MESH,
        )

    def forward_copy(c, p, way):
        rows = pl.ds(*PARTS[p])
        return pltpu.make_async_remote_copy(
            gath_hbm.at[1 + 2 * way, c, way, rows], gath_hbm.at[2, c, way, rows],
            fw_send.at[c, p, way], fw_recv.at[c, p, way], device_id=near[p][way], device_id_type=MESH,
        )

    def start_loads(c, carry):
        load(c, 0).start()
        load(c, 1).start()

        @pl.when(sec == 1)
        def _():
            cot_load(c).start()

        return carry

    lax.fori_loop(0, 1, start_loads, 0)
    load_w().start()
    lax.fori_loop(1, spans, start_loads, 0)
    list_v[0] = jnp.zeros((NB, 128), jnp.int32)
    list_v[0, :, 0:spans] = owner_ref[...] * ROWS_DEV + row_ref[...]

    greet([partner] + [d for pair in near for d in pair])
    list_copy(0, 0).start()
    list_copy(0, 1).start()

    def attend(c, slot):
        def names(h):
            heads = [slice((h * GROUP + g) * HDIM, (h * GROUP + g + 1) * HDIM) for g in range(GROUP)]
            return heads, slice(h * HDIM, (h + 1) * HDIM), slice((KV_HEADS + h) * HDIM, (KV_HEADS + h + 1) * HDIM)

        def front(h):
            heads, cols, vcols = names(h)
            q = jnp.concatenate([q_v[c, :, s] for s in heads], axis=0)
            k = kv_v[c, :, cols]
            v = kv_v[c, :, vcols]
            s = nt(k, q)
            g = jnp.concatenate([cot_v[0, c, :, s] for s in heads], axis=0)
            return q, g, k, s, nt(v, g)

        def middle(q, g, k, s, dp):
            peak = jnp.max(s, axis=0, keepdims=True)
            e = jnp.exp2((s - peak) * (scale * math.log2(math.e)))
            prob = e * (1.0 / jnp.sum(e, axis=0, keepdims=True))
            low = prob.astype(BF16)
            dot = jnp.sum(low.astype(F32) * dp, axis=0, keepdims=True)
            return q, g, k, low, (prob * (dp - dot)).astype(BF16)

        def back(h, q, g, k, low, ds):
            heads, cols, vcols = names(h)
            grad = (g.astype(F32) + tn(ds, k) * scale).astype(BF16)
            for i, col in enumerate(heads):
                ig_v[c, :, col] = grad[i * SPAN : (i + 1) * SPAN]
            kvg_v[slot, :, vcols] = nn(low, g).astype(BF16)
            kvg_v[slot, :, cols] = (nn(ds, q) * scale).astype(BF16)

        now = front(0)
        done = None
        for h in range(KV_HEADS):
            ahead = front(h + 1) if h + 1 < KV_HEADS else None
            ready = middle(*now)
            if done is not None:
                back(h - 1, *done)
            done, now = ready, ahead
        back(KV_HEADS - 1, *done)

    def spread_lists(t):
        for stage in range(3):

            @pl.when(t == 2 * stage)
            def _(stage=stage):
                list_copy(stage, 0).wait_recv()
                list_copy(stage, 2).start()

            @pl.when(t == 2 * stage + 1)
            def _(stage=stage):
                list_copy(stage, 1).wait_recv()
                list_copy(stage, 2).wait_recv()
                if stage < 2:
                    list_copy(stage + 1, 0).start()
                    list_copy(stage + 1, 1).start()

    def step(t, carry):
        c = t - (1 - sec)
        live = (c >= 0) & (c < spans)
        slot = lax.rem(c + 3, 3)

        @pl.when(live)
        def _():
            load(c, 0).wait()
            load(c, 1).wait()
            cot_load(c).wait()
            attend(c, slot)
            cot_send(c).start()
            out_copy(c).start()

            @pl.when(c == 0)
            def _():
                load_w().wait()

        s = t - LAG_SUM

        @pl.when((s >= 0) & (s < spans))
        def _():
            mine = nt(w_v[sec], kvg_v[lax.rem(s, 3)])
            proj_copy(s).wait_recv()
            for n in range(NB):
                gown_v[s, n] = (mine[:, n * NBLEN : (n + 1) * NBLEN] + xrecv_v[s, n].astype(F32)).astype(BF16)
            for p in range(3):
                for way in range(2):
                    gather_copy(s, p, way).start()
            own_copy(s).start()

        @pl.when(live)
        def _():
            other = nt(w_v[1 - sec], kvg_v[slot])
            for n in range(NB):
                xsend_v[c, n] = other[:, n * NBLEN : (n + 1) * NBLEN].astype(BF16)
            proj_copy(c).start()

        f = t - LAG_FWD

        @pl.when((f >= 0) & (f < spans))
        def _():
            for p in range(3):
                for way in range(2):
                    gather_copy(f, p, way).wait_recv()
                    forward_copy(f, p, way).start()

        spread_lists(t)

        @pl.when(t == spans + 1)
        def _():
            plan(list_v, table_ref, most_ref)

        return carry

    lax.fori_loop(0, spans + LAG_FWD, step, 0)

    def finish(c, carry):
        out_copy(c).wait()
        cot_send(c).wait_send()

        @pl.when(sec == 1)
        def _():
            pltpu.make_async_copy(og_hbm.at[c], cot_v.at[1, c], cot_sem.at[1, c]).wait()

        proj_copy(c).wait_send()
        own_copy(c).wait()
        for p in range(3):
            for way in range(2):
                gather_copy(c, p, way).wait_send()
                forward_copy(c, p, way).wait()
        return carry

    lax.fori_loop(0, spans, finish, 0)
    for stage in range(3):
        for hop in range(3):
            list_copy(stage, hop).wait_send()


def relay(queries, nb_kv, out_grad, weight, owners, rows):
    spans = nb_kv.shape[0]
    kvw2 = nb_kv.shape[-1]
    inner = queries.shape[-1]
    dma = pltpu.SemaphoreType.DMA
    item = (spans, NB, HALF, 128)
    any_spec = pl.BlockSpec(memory_space=pl.ANY)
    vmem_spec = pl.BlockSpec(memory_space=pltpu.VMEM)
    return pl.pallas_call(
        relay_kernel,
        name="relay",
        out_shape=(
            jax.ShapeDtypeStruct((spans, SPAN, inner), BF16),
            jax.ShapeDtypeStruct((RING,) + item, BF16),
            jax.ShapeDtypeStruct((24, 128), jnp.int32),
            jax.ShapeDtypeStruct((1, 1), jnp.int32),
        ),
        in_specs=[any_spec] * 4 + [vmem_spec] * 2,
        out_specs=(any_spec, any_spec, vmem_spec, pl.BlockSpec(memory_space=pltpu.SMEM)),
        scratch_shapes=[
            pltpu.VMEM((spans, SPAN, inner), BF16),
            pltpu.VMEM((spans, NB * NBLEN, kvw2), BF16),
            pltpu.VMEM((2, spans, SPAN, inner), BF16),
            pltpu.VMEM((spans, SPAN, inner), BF16),
            pltpu.VMEM((2, HALF, kvw2), BF16),
            pltpu.VMEM((3, NB * NBLEN, kvw2), BF16),
            pltpu.VMEM(item, BF16),
            pltpu.VMEM(item, BF16),
            pltpu.VMEM(item, BF16),
            pltpu.VMEM((RING**3, NB, 128), jnp.int32),
            dma((spans, 2)),
            dma(()),
            dma((spans,)),
            dma((spans,)),
            dma((2, spans)),
            dma((spans,)),
            dma((spans,)),
            dma((spans,)),
            dma((spans, 3, 2)),
            dma((spans, 3, 2)),
            dma((spans, 3, 2)),
            dma((spans, 3, 2)),
            dma((3, 3)),
            dma((3, 3)),
        ],
        compiler_params=pltpu.CompilerParams(
            collective_id=0, has_side_effects=True, vmem_limit_bytes=60 * 2**20
        ),
        cost_estimate=pl.CostEstimate(flops=7 * 10**9, bytes_accessed=20 * 10**6, transcendentals=2**21),
    )(
        queries.reshape(spans, SPAN, inner),
        nb_kv.reshape(spans, NB * NBLEN, kvw2),
        out_grad.reshape(spans, SPAN, inner),
        weight.reshape(2, HALF, kvw2),
        owners.T,
        rows.T,
    )


def route_kernel(cap, table, gath_hbm, out_ref, prefix, *refs):
    names = ("gath", "msend", "mrecv", "psend", "rtrans", "rrecv")
    count_of = len(PIECES)
    buf = {name: refs[count_of * i : count_of * (i + 1)] for i, name in enumerate(names)}
    sems = refs[count_of * len(names) :]
    ld_sem, sems = sems[0], [sems[1 + 2 * i : 3 + 2 * i] for i in range(6)]
    stay, slots, passed = cap
    total = RING * stay
    near = neighbours()
    base = 0 if cap == FAST else 12
    first, second = range(3), range(3, 6)

    def load(q):
        _, begin, size = PIECES[q]
        return pltpu.make_async_copy(gath_hbm.at[:, pl.ds(begin, size)], buf["gath"][q], ld_sem.at[q])

    def remote(q, way, axis, src, dst, kind):
        send, recv = sems[kind]
        return pltpu.make_async_remote_copy(
            src, dst, send.at[q, way], recv.at[q, way],
            device_id=near[(PIECES[q][0] + axis) % 3][way], device_id_type=MESH,
        )

    def mid_first(q, way):
        return remote(q, way, 1, buf["msend"][q].at[pl.ds(way * slots, passed)],
                      buf["mrecv"][q].at[pl.ds(stay + way * slots, passed)], 0)

    def mid_rest(q, way):
        rest = slots - passed
        return remote(q, way, 1, buf["msend"][q].at[pl.ds(way * slots + passed, rest)],
                      buf["mrecv"][q].at[pl.ds(stay + way * slots + passed, rest)], 1)

    def mid_pass(q, way):
        return remote(q, way, 1, buf["mrecv"][q].at[pl.ds(stay + way * slots, passed)],
                      buf["mrecv"][q].at[pl.ds(stay + 2 * slots + way * passed, passed)], 2)

    def far(q, way):
        return remote(q, way, 2, buf["psend"][q].at[pl.ds(32 + 8 * way, 8)], buf["rtrans"][q].at[way], 3)

    def near_now(q, way):
        d = 1 + 2 * way
        part = 8 * (1 - way)
        return remote(q, way, 2, buf["psend"][q].at[pl.ds(16 * d + part, 8)],
                      buf["rrecv"][q].at[way, pl.ds(part, 8)], 4)

    def near_late(q, way):
        d = 1 + 2 * way
        part = 8 * way
        return remote(q, way, 2, buf["psend"][q].at[pl.ds(16 * d + part, 8)],
                      buf["rrecv"][q].at[way, pl.ds(part, 8)], 5)

    for q in range(count_of):
        load(q).start()
    greet([d for pair in near for d in pair])
    prefix[total] = jnp.zeros(prefix.shape[1:], BF16)

    def fill(q, name, begin, number, entry):
        def body(j, carry):
            index = table[base + PIECES[q][0] * 4, entry + j]
            buf[name][q][begin + j] = buf["gath"][q][index]
            return carry

        lax.fori_loop(0, number, body, 0)

    def send_first(q):
        for way in range(2):
            fill(q, "msend", way * slots, passed, stay + way * slots)
            mid_first(q, way).start()

    def send_rest(q):
        if slots > passed:
            for way in range(2):
                fill(q, "msend", way * slots + passed, slots - passed, stay + way * slots + passed)
                mid_rest(q, way).start()

    def pass_on(q):
        for way in range(2):
            mid_first(q, way).wait_recv()
            mid_pass(q, way).start()

    def reduce(q):
        part, _, size = PIECES[q]
        for way in range(2):
            if slots > passed:
                mid_rest(q, way).wait_recv()
            mid_pass(q, way).wait_recv()

        def run(n, acc):
            value = buf["mrecv"][q][table[base + part * 4 + 1, n]].astype(F32)
            acc = acc * table[base + part * 4 + 2, n].astype(F32) + value
            prefix[n, pl.ds(0, size)] = acc.astype(BF16)
            return acc

        lax.fori_loop(0, total, run, jnp.zeros((size, 128), F32))

        def rows(d):
            def body(r, carry):
                index = table[base + part * 4 + 3, d * 16 + r]
                buf["psend"][q][d * 16 + r] = prefix[index, pl.ds(0, size)]
                return carry

            lax.fori_loop(0, ROWS_DEV, body, 0)

        rows(2)
        far(q, 0).start()
        far(q, 1).start()
        rows(1)
        near_now(q, 0).start()
        rows(3)
        near_now(q, 1).start()
        rows(0)

    def join(q):
        for way in range(2):
            far(q, way).wait_recv()
            start = 16 * (1 + 2 * way) + 8 * way

            def add(r, carry):
                buf["psend"][q][start + r] = (
                    buf["psend"][q][start + r].astype(F32) + buf["rtrans"][q][way, r].astype(F32)
                ).astype(BF16)
                return carry

            lax.fori_loop(0, 8, add, 0)
            near_late(q, way).start()

    def finish(q):
        _, begin, size = PIECES[q]
        for way in range(2):
            near_now(q, way).wait_recv()
            near_late(q, way).wait_recv()

        def final(r, carry):
            out_ref[r, pl.ds(begin, size)] = (
                buf["psend"][q][r].astype(F32)
                + buf["rrecv"][q][0, r].astype(F32)
                + buf["rrecv"][q][1, r].astype(F32)
            ).astype(BF16)
            return carry

        lax.fori_loop(0, ROWS_DEV, final, 0)

    for q in first:
        load(q).wait()
        send_first(q)
    for q in first:
        send_rest(q)
    for q in second:
        load(q).wait()
        send_first(q)
    for q in first:
        pass_on(q)
    for q in second:
        send_rest(q)
    for q in range(count_of):
        fill(q, "mrecv", 0, stay, 0)
    for q in second:
        pass_on(q)
    for q in range(count_of):
        reduce(q)
    for q in range(count_of):
        join(q)
    for q in range(count_of):
        finish(q)
    for q in range(count_of):
        for way in range(2):
            mid_first(q, way).wait_send()
            if slots > passed:
                mid_rest(q, way).wait_send()
            mid_pass(q, way).wait_send()
            far(q, way).wait_send()
            near_now(q, way).wait_send()
            near_late(q, way).wait_send()


def route(cap, ident, gathered, table):
    items = gathered.shape[0]
    stay, slots, passed = cap
    sizes = [size for _, _, size in PIECES]
    dma = pltpu.SemaphoreType.DMA

    def per_piece(*lead):
        return [pltpu.VMEM(lead + (size, 128), BF16) for size in sizes]

    return pl.pallas_call(
        functools.partial(route_kernel, cap),
        name="route%d" % slots,
        out_shape=jax.ShapeDtypeStruct((ROWS_DEV, HALF, 128), BF16),
        in_specs=[pl.BlockSpec(memory_space=pltpu.SMEM), pl.BlockSpec(memory_space=pl.ANY)],
        out_specs=pl.BlockSpec(memory_space=pltpu.VMEM),
        scratch_shapes=[pltpu.VMEM((RING * stay + 1, max(sizes), 128), BF16)]
        + per_piece(items)
        + per_piece(2 * slots)
        + per_piece(stay + 2 * slots + 2 * passed)
        + per_piece(64)
        + per_piece(2, 8)
        + per_piece(2, ROWS_DEV)
        + [dma((len(sizes),))]
        + [dma((len(sizes), 2))] * 12,
        compiler_params=pltpu.CompilerParams(
            collective_id=ident, has_side_effects=True, vmem_limit_bytes=60 * 2**20
        ),
        cost_estimate=pl.CostEstimate(flops=10**7, bytes_accessed=10**7, transcendentals=0),
    )(table, gathered)


def hand_out_kernel(grad, enc, grad_out, enc_out, grad_v, in_sem, out_sem, enc_sem):
    count_of = grad.shape[0]
    ins = [pltpu.make_async_copy(grad.at[i], grad_v.at[i], in_sem.at[i]) for i in range(count_of)]
    outs = [pltpu.make_async_copy(grad_v.at[i], grad_out.at[i], out_sem.at[i]) for i in range(count_of)]
    encs = []
    for i in range(4):
        some = pl.ds(i * (ROWS_DEV // 4), ROWS_DEV // 4)
        encs.append(pltpu.make_async_copy(enc.at[some], enc_out.at[some], enc_sem.at[i]))
    for copy in ins + encs:
        copy.start()
    for copy, out in zip(ins, outs):
        copy.wait()
        out.start()
    for copy in encs + outs:
        copy.wait()


def hand_out(grad, enc):
    any_spec = pl.BlockSpec(memory_space=pl.ANY)
    dma = pltpu.SemaphoreType.DMA
    return pl.pallas_call(
        hand_out_kernel,
        name="hand_out",
        out_shape=(jax.ShapeDtypeStruct(grad.shape, grad.dtype), jax.ShapeDtypeStruct(enc.shape, enc.dtype)),
        in_specs=[any_spec, pl.BlockSpec(memory_space=pltpu.VMEM)],
        out_specs=(any_spec,) * 2,
        scratch_shapes=[
            pltpu.VMEM(grad.shape, grad.dtype), dma((grad.shape[0],)), dma((grad.shape[0],)), dma((4,))
        ],
        compiler_params=pltpu.CompilerParams(vmem_limit_bytes=60 * 2**20),
        cost_estimate=pl.CostEstimate(flops=0, bytes_accessed=8 * 10**6, transcendentals=0),
    )(grad, enc)


def local(queries, nb_kv, out_grad, kv_weight, nb_owner, nb_row):
    input_grad, gathered, table, most = relay(queries[0], nb_kv[0], out_grad, kv_weight[0], nb_owner, nb_row)
    gathered = gathered.reshape(-1, HALF, 128)
    packed = lax.cond(
        most[0, 0] == 0,
        lambda t, g: route(FAST, 1, g, t),
        lambda t, g: route(FULL, 2, g, t),
        table,
        gathered,
    )
    input_grad, packed = hand_out(input_grad, packed)
    return (input_grad.reshape(queries.shape), packed.swapaxes(1, 2))


def solution(mesh):
    in_specs = (
        P("section", "ctx", None),
        P("section", "ctx", None, None, None),
        P("ctx", None),
        P("section", None, None),
        P("ctx", None),
        P("ctx", None),
    )
    out_specs = (P("section", "ctx", None), P("ctx", None, "section"))
    return jax.shard_map(local, mesh=mesh, in_specs=in_specs, out_specs=out_specs, check_vma=False)
```

time: 123 us -> 97 us (0.79)
  Pallas kernels: 106 us -> 95.6 us
  local copies, waits for them, and re-layouts: 7.02 us -> 0 us
  other arithmetic: 6.99 us -> 0 us
  between operations: 2.59 us -> 1.27 us
    pallas_call x1 -> x2, Pallas kernels: 59.1 us -> 50.2 us  [the longest x1 47 us: route(): pl.pallas_call(functools.partial(route_kernel, cap), name='route%d' % slo...]
    unnamed x2 -> x0, local copies, waits for them, and re-layouts: 4.39 us -> none
    reduce_sum x9 -> x0, other arithmetic: 2 us -> none  [the longest x3 0.66 us: most_slots(): most = jnp.maximum(most, jnp.max(jnp.sum(hits, axis=(p, 3))))]
    reduce_max x3 -> x0, other arithmetic: 1.98 us -> none  [most_slots(): most = jnp.maximum(most, jnp.max(jnp.sum(hits, axis=(p, 3))))]
    pallas_call x1, Pallas kernels: 47 us -> 45.4 us  [relay(): pl.pallas_call(relay_kernel, name='relay', out_shape=(jax.ShapeDtypeStruc...]
    another operation x16 -> x0, local copies, waits for them, and re-layouts: 1.24 us -> none  [the longest x9 0.73 us: along(): values = jnp.stack([own[axes[p][which]][p] for p in range(3)])]
where the time goes in v3:
time: 97 us; the launch traced here: 96.9 us
  Pallas kernels  95.6 us (99%)
  between operations  1.27 us (1%)
    pallas_call x1, Pallas kernels, route(): pl.pallas_call(functools.partial(route_kernel, cap), name='route%d' % slo...  47 us
    pallas_call x1, Pallas kernels, relay(): pl.pallas_call(relay_kernel, name='relay', out_shape=(jax.ShapeDtypeStruc...  45.4 us
    pallas_call x1, Pallas kernels, hand_out(): pl.pallas_call(hand_out_kernel, name='hand_out', out_shape=(jax.ShapeDtyp...  3.16 us

profile of v3, /device:TPU:0, one launch (start us, length us, event | category | flops | bytes accessed | tf_op | source)
XLA Modules:
  0.0 96.9 jit_solution(2504500992199449266)
XLA Ops:
  0.6 45.4 %relay.1 = (bf16[8,64,2048]{2,1,0:T(8,128)(2,1)}, bf16[4,8,2,448,128]{4,3,2,1,0:T(8,128)(2,1)}, s32[24,128]{1,0:T(8,128)S(1)}, s32[1,1]{1,0:T(1,128)}) custom-call(bf16[8,64,2048]{2,1,0:T(8,128)(2,1)} %bitcast.13, bf16[8,256,1024]{2,1,0:T(8,128)(2,1)} %bitcast.12, bf16[8,64,2048]{2,1,0:T(8,128)(2,1)} %bitcast.14, bf16[2,448,1024]{2,1,0:T(8,128)(2,1)} %bitcast.16, ...), custom_call_target="tpu_custom_call" | custom-call | flops 7000000000 | bytes 20000000 | tf_op jit(solution)/shard_map/relay/pallas_call | solution.py:407
  46.7 47.0 %conditional.1 = (bf16[16,448,128]{2,1,0:T(8,128)(2,1)S(1)}) conditional(s32[]{:T(128)} %bitcast.6, (s32[24,128]{1,0:T(8,128)S(1)}, bf16[64,448,128]{2,1,0:T(8,128)(2,1)}) %tuple.18, (s32[24,128]{1,0:T(8,128)S(1)}, bf16[64,448,128]{2,1,0:T(8,128)(2,1)}) %tuple.19), branch_computations={%region_0.0_spmd, %region_1.0_spmd} | conditional | flops 10000000 | bytes 10000008 | solution.py:701
  46.7 47.0 %route16.1 = bf16[16,448,128]{2,1,0:T(8,128)(2,1)S(1)} custom-call(s32[24,128]{1,0:T(8,128)S(1)} %get-tuple-element.13.table, bf16[64,448,128]{2,1,0:T(8,128)(2,1)} %get-tuple-element.14.gath_hbm), custom_call_target="tpu_custom_call" | custom-call | flops 10000000 | bytes 10000000 | tf_op jit(solution)/shard_map/cond/branch_1_fun/route16/pallas_call | solution.py:642
  93.7 3.2 %hand_out.1 = (bf16[8,64,2048]{2,1,0:T(8,128)(2,1)}, bf16[16,448,128]{2,1,0:T(8,128)(2,1)}) custom-call(bf16[8,64,2048]{2,1,0:T(8,128)(2,1)} %get-tuple-element.23.grad, bf16[16,448,128]{2,1,0:T(8,128)(2,1)S(1)} %get-tuple-element.29.enc), custom_call_target="tpu_custom_call" | custom-call | bytes 8000000 | tf_op jit(solution)/shard_map/hand_out/pallas_call | solution.py:684
